TPU v7x, 128 devices: a whole 4x4x4 slice. The times are simulated.
128 devices in a mesh: row: 8 (over x, core), col: 16 (over z, y).
Axes of the slice: x: 4, y: 4, z: 4, core: 2. Of those that a mesh axis runs over, the one named last changes fastest.
Arguments:
- initial: float32 [256, 128], replicated, may hold values from -6 to 6
- observed: float32 [16384, 64, 128], P(('row', 'col')), may hold values from -6 to 6
- mask: int32 [16384, 64], P(('row', 'col')), may hold values 0 or 1
- obs_map: float32 [64, 256], replicated, may hold values from -0.375 to 0.375
- weights: float32 [64], replicated, may hold values from 0.05 to 0.4
- transition: float32 [256, 256], replicated, may hold values from -1 to 1, as said below
Outputs:
- means: float32 [16384, 256, 128], P(('row', 'col'))
Inputs may be any that keep to these rules, and one draw needn't show every extreme that they name: `transition`: a positive diagonal below one; the absolute values of each row and of each column sum to at most one.
All inputs are finite; a program needn't handle non-finite values. No bound on the sum of `mask` on one device may be relied on, other than what follows from the above.
Results may differ from a plain program's by a relative error of at most 0.0003.
Values sent between devices are 32-bit elements; how exact they have to be, the bound alone decides.
A program may use at most 256 MiB of HBM per device.

v0:
```python
import jax
import jax.numpy as jnp
from jax import lax
from jax.sharding import PartitionSpec as P

highest = lax.Precision.HIGHEST


def carried_in(part, axis, combine, identity):
    place = lax.axis_index(axis)
    gathered = jax.tree.map(lambda a: lax.all_gather(a, axis), part)
    state = jax.tree.map(lambda a, e: jnp.zeros_like(a) + jnp.asarray(e, a.dtype), part, identity)

    def one(lap, state):
        return combine(
            state, jax.tree.map(lambda a: lax.dynamic_index_in_dim(a, lap, 0, False), gathered)
        )

    return lax.fori_loop(0, place, one, state)


def from_root(value, axis, root):
    mine = lax.axis_index(axis) == root
    return lax.psum(jnp.where(mine, value, jnp.zeros_like(value)), axis)


def product(left, right):
    return jnp.dot(left, right, precision=highest, preferred_element_type=jnp.float32)


def combine(earlier, later):
    return (product(later[0], earlier[0]), product(later[0], earlier[1]) + later[1])


def local(initial, observed, mask, obs_map, weights, transition):
    width = transition.shape[0]
    members = observed.shape[2]
    gain = obs_map.T * weights[None, :]
    mapped = product(obs_map, transition)
    masks = mask.astype(jnp.float32)
    unit = jnp.eye(width, dtype=jnp.float32)
    blank = jnp.zeros((width, members), jnp.float32)

    def step_maps(obs_now, mask_row):
        masked_gain = gain * mask_row[None, :]
        return (transition - product(masked_gain, mapped), product(masked_gain, obs_now))

    def forward(carry, inputs):
        advance, forcing = step_maps(inputs[0], inputs[1])
        prefix = product(advance, carry[0])
        local_mean = product(advance, carry[1]) + forcing
        return ((prefix, local_mean), (prefix, local_mean))

    (total, offset), (prefixes, local_means) = lax.scan(forward, (unit, blank), (observed, masks))
    identity = (unit, blank)
    before_col = carried_in((total, offset), "col", combine, identity)
    through = combine(before_col, (total, offset))
    joined = jnp.concatenate([through[0], through[1]], axis=1)
    row_sum = from_root(joined, "col", lax.axis_size("col") - 1)
    before_row = carried_in((row_sum[:, :width], row_sum[:, width:]), "row", combine, identity)
    carry_in = combine(before_row, before_col)
    start = product(carry_in[0], initial) + carry_in[1]
    means = local_means + jnp.einsum(
        "tij,jk->tik", prefixes, start, precision=highest, preferred_element_type=jnp.float32
    )
    return means


def solution(mesh):
    in_specs = (P(), P(("row", "col"), None, None), P(("row", "col"), None), P(), P(), P())
    out_specs = P(("row", "col"), None, None)
    return jax.shard_map(local, mesh=mesh, in_specs=in_specs, out_specs=out_specs, check_vma=False)
```

profile of v0, /device:TPU:6, one launch (start us, length us, event | category | flops | bytes accessed | tf_op | source)
XLA Modules:
  0.0 920.0 jit_solution(471225092316889969)
XLA Ops:
  9.8 577.2 %while.43 = (s32[]{:T(128)}, f32[256,256]{1,0:T(8,128)S(1)}, f32[256,128]{1,0:T(8,128)S(1)}, f32[128,256,256]{2,1,0:T(8,128)}, f32[128,256,128]{2,1,0:T(8,128)},...) while((s32[]{:T(128)}, f32[256,256]{1,0:T(8,128)S(1)}, ...), condition=%wide.region_1.2_spmd.clone, body=%wide.region_0.1_spmd.clone.sunk | while | flops 377651200 | bytes 3508867 | solution.py:54
  73.8 1.3 convolution_subtract_fusion.2
  109.9 1.3 convolution_subtract_fusion.2
  150.6 1.3 convolution_subtract_fusion.2
  159.6 1.3 convolution_subtract_fusion.2
  164.1 1.3 convolution_subtract_fusion.2
  168.7 1.3 convolution_subtract_fusion.2
  173.2 1.3 convolution_subtract_fusion.2
  204.7 1.3 convolution_subtract_fusion.2
  213.7 1.3 convolution_subtract_fusion.2
  254.3 1.3 convolution_subtract_fusion.2
  263.4 1.3 convolution_subtract_fusion.2
  267.9 1.3 convolution_subtract_fusion.2
  272.4 1.3 convolution_subtract_fusion.2
  285.9 1.3 convolution_subtract_fusion.2
  299.4 1.3 convolution_subtract_fusion.2
  335.5 1.3 convolution_subtract_fusion.2
  362.5 1.3 convolution_subtract_fusion.2
  376.0 1.3 convolution_subtract_fusion.2
  389.6 1.3 convolution_subtract_fusion.2
  412.1 1.3 convolution_subtract_fusion.2
  421.1 1.3 convolution_subtract_fusion.2
  443.7 1.3 convolution_subtract_fusion.2
  448.3 1.3 convolution_subtract_fusion.2
  457.3 1.3 convolution_subtract_fusion.2
  466.3 1.3 convolution_subtract_fusion.2
  470.8 1.3 convolution_subtract_fusion.2
  502.3 1.3 convolution_subtract_fusion.2
  511.3 1.3 convolution_subtract_fusion.2
  515.8 1.3 convolution_subtract_fusion.2
  524.9 1.3 convolution_subtract_fusion.2
  529.4 1.3 convolution_subtract_fusion.2
  547.4 1.3 convolution_subtract_fusion.2
  556.5 1.3 convolution_subtract_fusion.2
  579.0 1.3 convolution_subtract_fusion.2
  589.5 45.9 %all-gather.11.cloned.1.call-done = f32[4096,128]{1,0:T(8,128)} async-done(((f32[256,128]{1,0:T(8,128)}), f32[4096,128]{1,0:T(8,128)}) %all-gather.11.cloned.1.call-update) | async-done | bytes 2097168 | tf_op jit(solution)/shard_map/all_gather | solution.py:11
  635.4 53.1 %all-gather.9.cloned.1.call-done = f32[4096,256]{1,0:T(8,128)} async-done(((f32[256,256]{1,0:T(8,128)}), f32[4096,256]{1,0:T(8,128)}) %all-gather.9.cloned.1.call-update) | async-done | bytes 4194320 | tf_op jit(solution)/shard_map/all_gather | solution.py:11
  688.5 1.5 fusion.31
  690.1 1.3 convolution_add_fusion.5
  692.3 125.0 %all-reduce.2.cloned.1.call-done = f32[256,384]{0,1:T(8,128)} async-done(((f32[256,384]{0,1:T(8,128)}), f32[256,384]{0,1:T(8,128)}) %all-reduce.2.cloned.1.call-update) | async-done | bytes 393232 | tf_op jit(solution)/shard_map/psum | solution.py:24
  817.3 1.6 slice.9
  819.0 1.7 slice.8
  820.7 19.3 %all-gather.15.cloned.1.call-done = f32[2048,128]{0,1:T(8,128)} async-done(((f32[256,128]{0,1:T(8,128)}), f32[2048,128]{0,1:T(8,128)}) %all-gather.15.cloned.1.call-update) | async-done | bytes 1048592 | tf_op jit(solution)/shard_map/all_gather | solution.py:11
  840.0 2.5 copy.18
  842.5 24.8 %all-gather.13.cloned.1.call-done = f32[2048,256]{0,1:T(8,128)} async-done(((f32[256,256]{0,1:T(8,128)}), f32[2048,256]{0,1:T(8,128)}) %all-gather.13.cloned.1.call-update) | async-done | bytes 2097168 | tf_op jit(solution)/shard_map/all_gather | solution.py:11
  867.3 1.9 copy.17
  869.2 10.5 %while.42 = (s32[]{:T(128)}, f32[256,256]{1,0:T(8,128)S(1)}, f32[256,128]{1,0:T(8,128)S(1)}, s32[]{:T(128)}, f32[8,256,256]{2,1,0:T(8,128)S(1)}, /*index=5*/f32[...) while((s32[]{:T(128)}, f32[256,256]{1,0:T(8,128)S(1)}, f32[256,128]{1,0:T(8,128)S(1)}, s32[]{:T(128)}, ...), condition=%wide.region_6.7_spmd, body=%wide.region_5.6_spmd.sunk | while | flops 302022656 | bytes 2229379 | solution.py:19
  880.9 32.5 %convolution_add_fusion.3 = f32[128,256,128]{2,1,0:T(8,128)} fusion(f32[128,256,128]{2,1,0:T(8,128)} %get-tuple-element.128, f32[128,256,256]{2,1,0:T(8,128)} %get-tuple-element.129, f32[256,128,1]{1,0,2:T(8,128)S(1)} %fusion.28), kind=kOutput, calls=%fused_computation.34 | convolution fusion | flops 12889096192 | bytes 67239936 | tf_op jit(solution)/shard_map/tij,jk->tik/dot_general | solution.py:63
  (923 shorter events, 546.4 us)
Async XLA Ops:
  6.5 873.6 %copy-start = (f32[256,128]{1,0:T(8,128)S(1)}, f32[256,128]{1,0:T(8,128)}, u32[]{:S(2)}) copy-start(f32[256,128]{1,0:T(8,128)} %param.12) | copy-start | bytes 393220
  6.5 628.9 %all-gather.11.cloned.1.call-start = ((), (), s32[]{:S(2)}) async-start(), calls=%async_computation.2 | async-start | bytes 2228224 | tf_op jit(solution)/shard_map/all_gather | solution.py:11
  587.0 0.7 copy-start.3
  587.0 0.8 copy-start.2
  587.7 100.8 %all-gather.9.cloned.1.call-start = ((), (), s32[]{:S(2)}) async-start(), calls=%async_computation.1 | async-start | bytes 4456448 | tf_op jit(solution)/shard_map/all_gather | solution.py:11
  588.4 228.9 %all-reduce.2.cloned.1.call-start = ((), (), s32[]{:S(2)}) async-start(), calls=%async_computation | async-start | bytes 786432 | tf_op jit(solution)/shard_map/psum | solution.py:24
  692.3 147.7 %all-gather.15.cloned.1.call-start = ((), (), s32[]{:S(2)}) async-start(), calls=%async_computation.4 | async-start | bytes 1179648 | tf_op jit(solution)/shard_map/all_gather | solution.py:11
  818.9 48.3 %all-gather.13.cloned.1.call-start = ((), (), s32[]{:S(2)}) async-start(), calls=%async_computation.3 | async-start | bytes 2359296 | tf_op jit(solution)/shard_map/all_gather | solution.py:11
  880.9 32.5 %copy-start.1 = (f32[256,128]{1,0:T(8,128)S(1)}, f32[256,128]{1,0:T(8,128)}, u32[]{:S(2)}) copy-start(f32[256,128]{1,0:T(8,128)} %param.12) | copy-start | bytes 393220
Sparse Core Ops, SparseCore 0:
  587.8 47.6 all-gather.10
  637.6 50.8 all-gather.8
  692.4 124.9 all-reduce.1
  819.1 20.8 all-gather.14
  841.5 25.7 all-gather.12
where the time goes:
time: 936 us; the launch traced here: 920 us
  matrix products  616 us (66%)
  waiting for transfers between devices  269 us (29%)
  local copies, waits for them, and re-layouts  15 us (2%)
  between operations  13.3 us (1%)
    dot_general x530, matrix products, product(): jnp.dot(left, right, precision=highest, preferred_element_type=jnp.float32)  584 us
    all_gather x4, waiting for transfers between devices, carried_in(): gathered = jax.tree.map(lambda a: lax.all_gather(a, axis), part)  143 us
    psum x1, waiting for transfers between devices, from_root(): return lax.psum(jnp.where(mine, value, jnp.zeros_like(value)), axis)  125 us
    dot_general x1, matrix products, local(): jnp.einsum('tij,jk->tik', prefixes, start, precision=highest, preferred_e...  32.5 us
  transfers between devices with their start and end apart: 5, of which 5 were waited for; matrix products, arithmetic and copies ran while one was open for 1% of the time, Pallas kernels for 0%

commit v1 on v0

v1 whole, which is shorter than its diff:
```python
import jax
import jax.numpy as jnp
from jax import lax
from jax.experimental import pallas as pl
from jax.experimental.pallas import tpu as pltpu
from jax.sharding import PartitionSpec as P

MESH = pl.DeviceIdType.MESH
VMEM = pltpu.VMEM
D, OBS, E = 256, 64, 128
WIDE = D + E
LEN = 8
GROUP = 4
F32, BF16 = jnp.float32, jnp.bfloat16


def exact(left, right):
    return jnp.dot(left, right, precision=lax.Precision.HIGHEST, preferred_element_type=F32)


def exact_nt(left, right):
    return lax.dot_general(
        left, right, (((1,), (1,)), ((), ())), precision=lax.Precision.HIGHEST, preferred_element_type=F32
    )


def fast(left, right):
    return jnp.dot(left, right, preferred_element_type=F32)


def split(value):
    high = value.astype(BF16)
    return high, (value - high.astype(F32)).astype(BF16)


def three(left, right):
    return fast(left[0], right[0]) + fast(left[0], right[1]) + fast(left[1], right[0])


def four_wide(value):
    high, low = split(value)
    return jnp.concatenate([high, high, low, low], axis=1)


def four_tall(parts):
    high, low = parts
    return jnp.concatenate([high, low, high, low], axis=0)


def unit(size):
    rows = lax.broadcasted_iota(jnp.int32, (size, size), 0)
    return (rows == lax.broadcasted_iota(jnp.int32, (size, size), 1)).astype(F32)


def compose(later, earlier):
    joined = exact(later[:, :D], earlier)
    return jnp.concatenate([joined[:, :D], joined[:, D:] + later[:, D:]], axis=1)


def maps_kernel(
    mask_ref, obs_ref, map_ref, weight_ref, trans_ref, left_ref, top_ref, root_ref,
    power, seen, lags, couple_hi, couple_lo, back_hi, back_lo, group_map,
):
    turn = pl.program_id(0)

    @pl.when(turn == 0)
    def _prepare():
        trans = trans_ref[...]
        two = exact(trans, trans)
        four = exact(two, two)
        power[...] = exact(four, four)
        one_seen = exact(map_ref[...], trans)
        seen[0:OBS, :] = one_seen
        seen[OBS:2 * OBS, :] = exact(one_seen, trans)
        seen[2 * OBS:4 * OBS, :] = exact(seen[0:2 * OBS, :], two)
        seen[4 * OBS:8 * OBS, :] = exact(seen[0:4 * OBS, :], four)
        gain = exact_nt(unit(D), map_ref[...]) * weight_ref[...]
        stack = exact(seen[...], gain)
        lags[...] = four_wide(stack[0:3 * OBS, :])
        high, low = split(stack)
        for j in range(4):
            couple_hi[:, OBS * j:OBS * (j + 1)] = high[OBS * (3 - j):OBS * (7 - j), :]
            couple_lo[:, OBS * j:OBS * (j + 1)] = low[OBS * (3 - j):OBS * (7 - j), :]
        pair = jnp.concatenate([exact(trans, gain), gain], axis=1)
        quad = jnp.concatenate([exact(two, pair), pair], axis=1)
        whole = jnp.concatenate([exact(four, quad), quad], axis=1)
        high, low = split(whole)
        back_hi[...] = high
        back_lo[...] = low

    masks = pltpu.roll(mask_ref[...].astype(F32), 128 - turn * (LEN * GROUP), 1)
    lag = lags[...]
    couple = (couple_hi[...], couple_lo[...])
    done = []
    ahead = None
    for half in range(2):
        part = []
        wait = [None] * 4
        for s in range(4):
            step = half * 4 + s
            seen_now = seen[OBS * step:OBS * (step + 1), :]
            right = jnp.concatenate(
                [v for i in range(GROUP) for v in (seen_now, -obs_ref[LEN * i + step])], axis=1
            )
            if ahead is not None:
                right = right - ahead[OBS * s:OBS * (s + 1), :]
            if wait[s] is not None:
                right = right - wait[s]
            keep = jnp.concatenate(
                [
                    jnp.broadcast_to(masks[:, LEN * i + step:LEN * i + step + 1], (OBS, WIDE))
                    for i in range(GROUP)
                ],
                axis=1,
            )
            found = split(right * keep)
            part.append(found)
            if s < 3:
                push = fast(lag[0:OBS * (3 - s), :], four_tall(found))
                for later in range(s + 1, 4):
                    term = push[OBS * (later - s - 1):OBS * (later - s), :]
                    wait[later] = term if wait[later] is None else wait[later] + term
        half_hi = jnp.concatenate([p[0] for p in part], axis=0)
        half_lo = jnp.concatenate([p[1] for p in part], axis=0)
        done.append((half_hi, half_lo))
        if half == 0:
            ahead = three(couple, done[0])
    total = three((back_hi[:, 0:D], back_lo[:, 0:D]), done[0])
    total = total + three((back_hi[:, D:2 * D], back_lo[:, D:2 * D]), done[1])
    leaf = []
    for i in range(GROUP):
        mine = total[:, WIDE * i:WIDE * (i + 1)]
        leaf.append(jnp.concatenate([power[...] - mine[:, :D], -mine[:, D:]], axis=1))
    first = compose(leaf[1], leaf[0])
    second = compose(leaf[3], leaf[2])
    left_ref[0, 0] = leaf[0]
    left_ref[0, 1] = leaf[2]
    left_ref[0, 2] = first
    group_map[turn] = compose(second, first)

    @pl.when(turn == pl.num_programs(0) - 1)
    def _join():
        early = compose(group_map[1], group_map[0])
        late = compose(group_map[3], group_map[2])
        top_ref[0] = group_map[0]
        top_ref[1] = group_map[2]
        top_ref[2] = early
        whole = compose(late, early)
        for j in range(3):
            root_ref[j] = whole[:, E * j:E * (j + 1)]


def local_maps(mask_t, observed, obs_map, weights, transition):
    steps = observed.shape[0]
    turns = steps // (LEN * GROUP)

    def whole(shape):
        return pl.BlockSpec(shape, lambda i: (0,) * len(shape))

    return pl.pallas_call(
        maps_kernel,
        grid=(turns,),
        in_specs=[
            whole((OBS, steps)),
            pl.BlockSpec((LEN * GROUP, OBS, E), lambda i: (i, 0, 0)),
            whole((OBS, D)),
            whole((1, OBS)),
            whole((D, D)),
        ],
        out_specs=[
            pl.BlockSpec((1, 3, D, WIDE), lambda i: (i, 0, 0, 0)),
            whole((3, D, WIDE)),
            whole((3, D, E)),
        ],
        out_shape=[
            jax.ShapeDtypeStruct((turns, 3, D, WIDE), F32),
            jax.ShapeDtypeStruct((3, D, WIDE), F32),
            jax.ShapeDtypeStruct((3, D, E), F32),
        ],
        scratch_shapes=[
            VMEM((D, D), F32),
            VMEM((LEN * OBS, D), F32),
            VMEM((3 * OBS, 4 * OBS), BF16),
            VMEM((D, D), BF16),
            VMEM((D, D), BF16),
            VMEM((D, 2 * D), BF16),
            VMEM((D, 2 * D), BF16),
            VMEM((turns, D, WIDE), F32),
        ],
        compiler_params=pltpu.CompilerParams(
            dimension_semantics=("arbitrary",), vmem_limit_bytes=50 * 1024 * 1024
        ),
    )(mask_t, observed, obs_map, weights, transition)


def scan_kernel(
    own_ref, init_ref, start_ref,
    y_near, y_far, y_pair, y_all, z_near, z_far, z_pair, z_all,
    core_near, core_all, x_in, x_row, x_z, x_zs, x_y, send, recv,
):
    row, col = lax.axis_index("row"), lax.axis_index("col")
    x, core, z, y = row // 2, row % 2, col // 4, col % 4
    corner = jnp.logical_and(z == 3, y == 3)

    def remote(src, dst, out_sem, in_sem, device):
        return pltpu.make_async_remote_copy(
            src_ref=src, dst_ref=dst, send_sem=send.at[out_sem], recv_sem=recv.at[in_sem],
            device_id=device, device_id_type=MESH,
        )

    barrier = pltpu.get_barrier_semaphore()

    def greet(device):
        pl.semaphore_signal(barrier, inc=1, device_id=device, device_id_type=MESH)

    for k in range(1, 4):
        greet((row, z * 4 + (y + k) % 4))

    @pl.when(y == 3)
    def _():
        for k in range(1, 4):
            greet((row, ((z + k) % 4) * 4 + y))

    @pl.when(corner)
    def _():
        greet((row + 1 - 2 * core, col))

    @pl.when(jnp.logical_and(corner, x > 0))
    def _():
        greet((row - 2, col))

    @pl.when(jnp.logical_and(corner, x < 3))
    def _():
        greet((row + 2, col))

    last_y = jnp.where(y == 3, 1, 0)
    last = last_y * jnp.where(z == 3, 1, 0)
    met = 3 + 3 * last_y + last * (1 + jnp.where(x > 0, 1, 0) + jnp.where(x < 3, 1, 0))
    pl.semaphore_wait(barrier, met)

    def apply(later, state):
        return exact(jnp.concatenate([later[0], later[1]], axis=1), state) + later[2]

    def join(later, block, j):
        got = exact(jnp.concatenate([later[0], later[1]], axis=1), block)
        return got + later[2] if j == 2 else got

    def level(place, at, own, near, far, pair, all_, base):
        def near_copy(j, to):
            return remote(own.at[j], near.at[j], base + j, base + j, at(to))

        def far_copy(src, j, to, slot):
            return remote(src.at[j], far.at[j], base + slot + j, base + 3 + j, at(to))

        @pl.when(place == 0)
        def _():
            for j in range(3):
                near_copy(j, 1).start()
            for j in range(3):
                far_copy(far, j, 3, 3).wait_recv()
                far_copy(far, j, 3, 3).start()
            for j in range(3):
                near_copy(j, 1).wait_send()
                far_copy(far, j, 3, 3).wait_send()

        @pl.when(place == 1)
        def _():
            for j in range(3):
                near_copy(j, 2).wait_recv()
                all_[j] = join(own, near[j], j)
                far_copy(all_, j, 2, 3).start()
                far_copy(all_, j, 0, 6).start()
            for j in range(3):
                far_copy(all_, j, 2, 3).wait_send()
                far_copy(all_, j, 0, 6).wait_send()

        @pl.when(place == 2)
        def _():
            for j in range(3):
                near_copy(j, 3).start()
            for j in range(3):
                far_copy(far, j, 3, 3).wait_recv()
            for j in range(3):
                near_copy(j, 3).wait_send()

        @pl.when(place == 3)
        def _():
            for j in range(3):
                near_copy(j, 2).wait_recv()
                pair[j] = join(own, near[j], j)
            for j in range(3):
                far_copy(far, j, 2, 3).wait_recv()
                all_[j] = join(pair, far[j], j)

    level(y, lambda p: (row, z * 4 + p), own_ref, y_near, y_far, y_pair, y_all, 0)

    @pl.when(y == 3)
    def _():
        level(z, lambda p: (row, p * 4 + 3), y_all, z_near, z_far, z_pair, z_all, 9)
        for j in range(3):
            y_pair[j] = join(y_near, y_far[j], j)

    def core_copy(j):
        return remote(z_all.at[j], core_near.at[j], 18 + j, 18 + j, (row + 1 - 2 * core, col))

    def chain_copy():
        return remote(x_z, x_in, 21, 21, (row + 2, col))

    def back_copy():
        return remote(x_in, x_row, 22, 22, (row + 1 - 2 * core, col))

    def z_copy(to, slot):
        return remote(x_row, x_z, slot, 23, (row, to * 4 + 3))

    def y_copy(to, slot):
        return remote(x_zs, x_y, slot, 24, (row, z * 4 + to))

    @pl.when(corner)
    def _():
        @pl.when(core == 0)
        def _():
            for j in range(3):
                core_copy(j).start()
            for j in range(3):
                z_pair[j] = join(z_near, z_far[j], j)

            @pl.when(x == 0)
            def _():
                x_row[...] = init_ref[...]

            @pl.when(x > 0)
            def _():
                back_copy().wait_recv()

            for j in range(3):
                core_copy(j).wait_send()

        @pl.when(core == 1)
        def _():
            for j in range(3):
                core_copy(j).wait_recv()
                core_all[j] = join(z_all, core_near[j], j)
            for j in range(3):
                z_pair[j] = join(z_near, z_far[j], j)

            @pl.when(x == 0)
            def _():
                x_in[...] = init_ref[...]

            @pl.when(x > 0)
            def _():
                chain_copy().wait_recv()
                back_copy().start()

            @pl.when(x < 3)
            def _():
                x_z[...] = apply(core_all, x_in[...])
                chain_copy().start()

            x_row[...] = apply(core_near, x_in[...])

            @pl.when(x > 0)
            def _():
                back_copy().wait_send()

            @pl.when(x < 3)
            def _():
                chain_copy().wait_send()

        for to in range(3):
            z_copy(to, 22 + 1 + to).start()
        x_zs[...] = apply(z_pair, x_row[...])
        for to in range(3):
            z_copy(to, 22 + 1 + to).wait_send()

    @pl.when(jnp.logical_and(y == 3, z != 3))
    def _():
        z_copy(0, 23).wait_recv()

        @pl.when(z == 0)
        def _():
            x_zs[...] = x_z[...]

        @pl.when(z == 1)
        def _():
            x_zs[...] = apply(z_near, x_z[...])

        @pl.when(z == 2)
        def _():
            x_zs[...] = apply(z_far, x_z[...])

    @pl.when(y == 3)
    def _():
        for to in range(3):
            y_copy(to, 26 + to).start()
        start_ref[...] = apply(y_pair, x_zs[...])
        for to in range(3):
            y_copy(to, 26 + to).wait_send()

    @pl.when(y != 3)
    def _():
        y_copy(0, 26).wait_recv()

        @pl.when(y == 0)
        def _():
            start_ref[...] = x_y[...]

        @pl.when(y == 1)
        def _():
            start_ref[...] = apply(y_near, x_y[...])

        @pl.when(y == 2)
        def _():
            start_ref[...] = apply(y_far, x_y[...])


def carried_in(root, initial):
    whole = pl.BlockSpec(memory_space=VMEM)
    return pl.pallas_call(
        scan_kernel,
        in_specs=[whole, whole],
        out_specs=whole,
        out_shape=jax.ShapeDtypeStruct((D, E), F32),
        scratch_shapes=[VMEM((3, D, E), F32)] * 10
        + [VMEM((D, E), F32)] * 5
        + [pltpu.SemaphoreType.DMA((29,)), pltpu.SemaphoreType.DMA((25,))],
        compiler_params=pltpu.CompilerParams(
            collective_id=0, has_side_effects=True, vmem_limit_bytes=16 * 1024 * 1024
        ),
    )(root, initial)


def means_kernel(
    start_ref, left_ref, top_ref, mask_ref, obs_ref, map_ref, weight_ref, trans_ref, out_ref,
    state, both_hi, both_lo, gains, held, sems,
):
    chunks = out_ref.shape[0]
    groups = chunks // GROUP
    both = jnp.concatenate([trans_ref[...], exact(map_ref[...], trans_ref[...])], axis=0)
    high, low = split(both)
    both_hi[...] = high
    both_lo[...] = low
    gains[...] = four_wide(exact_nt(unit(D), map_ref[...]) * weight_ref[...])

    def apply(later, value):
        return exact(later[:, :D], value) + later[:, D:]

    begin = [None] * groups
    begin[0] = start_ref[...]
    begin[2] = apply(top_ref[2], begin[0])
    begin[1] = apply(top_ref[0], begin[0])
    begin[3] = apply(top_ref[1], begin[2])
    for g in range(groups):
        third = apply(left_ref[g, 2], begin[g])
        second = apply(left_ref[g, 0], begin[g])
        state[g] = jnp.concatenate([begin[g], second, third, apply(left_ref[g, 1], third)], axis=1)

    def copy(s):
        slot = lax.rem(s, 2)
        return pltpu.make_async_copy(held.at[slot], out_ref.at[:, s], sems.at[slot])

    def step(s, carry):
        slot = lax.rem(s, 2)
        masks = pltpu.roll(mask_ref[...].astype(F32), 128 - s, 1)

        @pl.when(s >= 2)
        def _():
            copy(s - 2).wait()

        for g in range(groups):
            moved = three((both_hi[...], both_lo[...]), split(state[g]))
            seen = jnp.concatenate(
                [obs_ref[LEN * (GROUP * g + i) + s] for i in range(GROUP)], axis=1
            )
            keep = jnp.concatenate(
                [
                    jnp.broadcast_to(masks[:, LEN * (GROUP * g + i):LEN * (GROUP * g + i) + 1], (OBS, E))
                    for i in range(GROUP)
                ],
                axis=1,
            )
            found = (moved[D:, :] - seen) * keep
            now = moved[:D, :] - fast(gains[...], four_tall(split(found)))
            state[g] = now
            for i in range(GROUP):
                held[slot, GROUP * g + i] = now[:, E * i:E * (i + 1)]
        copy(s).start()
        return carry

    lax.fori_loop(0, LEN, step, 0)
    copy(LEN - 2).wait()
    copy(LEN - 1).wait()


def means_of(start, left, top, mask_t, observed, obs_map, weights, transition):
    steps = observed.shape[0]
    chunks = steps // LEN
    whole = pl.BlockSpec(memory_space=VMEM)
    out = pl.pallas_call(
        means_kernel,
        in_specs=[whole] * 8,
        out_specs=pl.BlockSpec(memory_space=pl.ANY),
        out_shape=jax.ShapeDtypeStruct((chunks, LEN, D, E), F32),
        scratch_shapes=[
            VMEM((chunks // GROUP, D, GROUP * E), F32),
            VMEM((D + OBS, D), BF16),
            VMEM((D + OBS, D), BF16),
            VMEM((D, 4 * OBS), BF16),
            VMEM((2, chunks, D, E), F32),
            pltpu.SemaphoreType.DMA((2,)),
        ],
        compiler_params=pltpu.CompilerParams(vmem_limit_bytes=50 * 1024 * 1024),
    )(start, left, top, mask_t, observed, obs_map, weights, transition)
    return out.reshape(steps, D, E)


def local(initial, observed, mask, obs_map, weights, transition):
    mask_t = mask.T
    row = weights.reshape(1, OBS)
    left, top, root = local_maps(mask_t, observed, obs_map, row, transition)
    start = carried_in(root, initial)
    return means_of(start, left, top, mask_t, observed, obs_map, row, transition)


def solution(mesh):
    in_specs = (P(), P(("row", "col"), None, None), P(("row", "col"), None), P(), P(), P())
    out_specs = P(("row", "col"), None, None)
    return jax.shard_map(local, mesh=mesh, in_specs=in_specs, out_specs=out_specs, check_vma=False)
```

time: 936 us -> 129 us (0.14); the launches traced: 920 us -> 127 us
  matrix products: 616 us -> 0 us
  waiting for transfers between devices: 269 us -> 0 us
  Pallas kernels: 0 us -> 122 us
  between operations: 13.3 us -> 0.2 us
  local copies, waits for them, and re-layouts: 15 us -> 4.1 us
    dot_general x531 -> x0, matrix products: 616 us -> none  [the longest x530 584 us: product(): jnp.dot(left, right, precision=highest, preferred_element_type=jnp.float32)]
    all_gather x4 -> x0, waiting for transfers between devices: 143 us -> none  [carried_in(): gathered = jax.tree.map(lambda a: lax.all_gather(a, axis), part)]
    psum x1 -> x0, waiting for transfers between devices: 125 us -> none  [from_root(): return lax.psum(jnp.where(mine, value, jnp.zeros_like(value)), axis)]
    pallas_call x0 -> x3, Pallas kernels: none -> 122 us  [the longest x1 69.6 us: carried_in(): pl.pallas_call(scan_kernel, in_specs=[whole, whole], out_specs=whole, out...]
  transfers between devices with their start and end apart: 5 -> 0, of which waited for: 5 -> 0; matrix products, arithmetic and copies ran while one was open for 1% -> 0% of each run, Pallas kernels for 0% -> 0%
where the time goes in v1:
time: 129 us; the launch traced here: 127 us
  Pallas kernels  122 us (95%)
  local copies, waits for them, and re-layouts  4.1 us (3%)
    pallas_call x1, Pallas kernels, carried_in(): pl.pallas_call(scan_kernel, in_specs=[whole, whole], out_specs=whole, out...  69.6 us
    pallas_call x1, Pallas kernels, means_of(): pl.pallas_call(means_kernel, in_specs=[whole] * 8, out_specs=pl.BlockSpec...  26.8 us
    pallas_call x1, Pallas kernels, local_maps(): pl.pallas_call(maps_kernel, grid=(turns,), in_specs=[whole((OBS, steps)),...  25.8 us
    unnamed x10, local copies, waits for them, and re-layouts  4.1 us

profile of v1, /device:TPU:6, one launch (start us, length us, event | category | flops | bytes accessed | tf_op | source)
XLA Modules:
  0.0 126.5 jit_solution(7838555333878788068)
XLA Ops:
  0.0 0.0 copy-start
  0.0 0.9 copy-done
  1.0 0.0 copy-start.1
  1.0 0.8 copy-done.1
  1.8 0.0 copy-start.2
  1.8 0.8 copy-done.2
  2.5 0.0 copy-start.4
  2.6 0.7 copy-done.4
  3.2 25.8 %shard_map.64 = (f32[4,3,256,384]{3,2,1,0:T(8,128)}, f32[3,256,384]{2,1,0:T(8,128)S(1)}, f32[3,256,128]{2,1,0:T(8,128)S(1)}) custom-call(s32[64,128]{1,0:T(8,128)S(1)} %bitcast.3, f32[128,64,128]{2,1,0:T(8,128)} %obs_ref.3, f32[64,256]{1,0:T(8,128)S(1)} %copy-done.1, f32[1,64]{1,0:T(1,128)S(1)} %bitcast.5, f32[256,256]{1,0:T(8,128)S(1)} %copy-done), custom_call_target="tpu_custom_call" | custom-call | tf_op jit(solution)/shard_map/pallas_call | solution.py:160
  29.1 0.0 copy-start.3
  29.1 0.9 copy-done.3
  30.0 69.6 %shard_map.65.start_ref = f32[256,128]{1,0:T(8,128)S(1)} custom-call(f32[3,256,128]{2,1,0:T(8,128)S(1)} %get-tuple-element.8.own_ref, f32[256,128]{1,0:T(8,128)S(1)} %copy-done.3), custom_call_target="tpu_custom_call" | custom-call | tf_op jit(solution)/shard_map/pallas_call | solution.py:419
  99.6 26.8 %shard_map.66 = f32[16,8,256,128]{3,2,1,0:T(8,128)} custom-call(f32[256,128]{1,0:T(8,128)S(1)} %shard_map.65.start_ref, f32[4,3,256,384]{3,2,1,0:T(8,128)} %get-tuple-element.9.left_ref, f32[3,256,384]{2,1,0:T(8,128)S(1)} %get-tuple-element.10.top_ref, s32[64,128]{1,0:T(8,128)S(1)} %bitcast.4, f32[128,64,128]{2,1,0:T(8,128)} %obs_ref.3, ...), custom_call_target="tpu_custom_call" | custom-call | tf_op jit(solution)/shard_map/pallas_call | solution.py:499
Async XLA Ops:
  0.0 0.9 copy-start
  1.0 0.8 copy-start.1
  1.8 0.8 copy-start.2
  2.5 0.7 copy-start.4
  29.1 0.9 copy-start.3

commit v2 on v1

--- a/solution.py
+++ b/solution.py
@@ -35,6 +35,10 @@
 
 def three(left, right):
     return fast(left[0], right[0]) + fast(left[0], right[1]) + fast(left[1], right[0])
+
+
+def four(left, right):
+    return three(left, right) + fast(left[1], right[1])
 
 
 def four_wide(value):
@@ -125,8 +129,8 @@
         done.append((half_hi, half_lo))
         if half == 0:
             ahead = three(couple, done[0])
-    total = three((back_hi[:, 0:D], back_lo[:, 0:D]), done[0])
-    total = total + three((back_hi[:, D:2 * D], back_lo[:, D:2 * D]), done[1])
+    total = four((back_hi[:, 0:D], back_lo[:, 0:D]), done[0])
+    total = total + four((back_hi[:, D:2 * D], back_lo[:, D:2 * D]), done[1])
     leaf = []
     for i in range(GROUP):
         mine = total[:, WIDE * i:WIDE * (i + 1)]
@@ -146,8 +150,7 @@
         top_ref[1] = group_map[2]
         top_ref[2] = early
         whole = compose(late, early)
-        for j in range(3):
-            root_ref[j] = whole[:, E * j:E * (j + 1)]
+        root_ref[...] = whole.T
 
 
 def local_maps(mask_t, observed, obs_map, weights, transition):
@@ -170,12 +173,12 @@
         out_specs=[
             pl.BlockSpec((1, 3, D, WIDE), lambda i: (i, 0, 0, 0)),
             whole((3, D, WIDE)),
-            whole((3, D, E)),
+            whole((WIDE, D)),
         ],
         out_shape=[
             jax.ShapeDtypeStruct((turns, 3, D, WIDE), F32),
             jax.ShapeDtypeStruct((3, D, WIDE), F32),
-            jax.ShapeDtypeStruct((3, D, E), F32),
+            jax.ShapeDtypeStruct((WIDE, D), F32),
         ],
         scratch_shapes=[
             VMEM((D, D), F32),
@@ -193,20 +196,68 @@
     )(mask_t, observed, obs_map, weights, transition)
 
 
+RISE = 64
+PARTS = WIDE // RISE
+MATRIX = D // RISE
+MEMBERS = 32
+TURNS = E // MEMBERS
+
+
+def cut(value):
+    high = value.astype(BF16)
+    rest = value - high.astype(F32)
+    middle = rest.astype(BF16)
+    return high, middle, (rest - middle.astype(F32)).astype(BF16)
+
+
 def scan_kernel(
     own_ref, init_ref, start_ref,
-    y_near, y_far, y_pair, y_all, z_near, z_far, z_pair, z_all,
-    core_near, core_all, x_in, x_row, x_z, x_zs, x_y, send, recv,
+    y_near, y_far, y_pair, y_all, z_near, z_far, z_pair, z_all, core_near, core_all, y_before, z_before,
+    x_in, x_next, x_row, x_z, x_zs, x_y,
+    own_cut, y_cut, z_cut, pair_cut, core_cut, chain_cut, side_cut, send, recv,
 ):
     row, col = lax.axis_index("row"), lax.axis_index("col")
     x, core, z, y = row // 2, row % 2, col // 4, col % 4
     corner = jnp.logical_and(z == 3, y == 3)
-
-    def remote(src, dst, out_sem, in_sem, device):
-        return pltpu.make_async_remote_copy(
-            src_ref=src, dst_ref=dst, send_sem=send.at[out_sem], recv_sem=recv.at[in_sem],
-            device_id=device, device_id_type=MESH,
-        )
+    used = {"send": 0, "recv": 0}
+
+    def lane(name, src, dst, device, parts, size, into=None):
+        first = used["send"]
+        used["send"] += parts
+        if into is None:
+            into = used["recv"]
+            used["recv"] += parts
+
+        def make(k):
+            rows = pl.ds(size * k, size)
+            return pltpu.make_async_remote_copy(
+                src_ref=src.at[rows], dst_ref=dst.at[rows],
+                send_sem=send.at[first + k], recv_sem=recv.at[into + k],
+                device_id=device, device_id_type=MESH,
+            )
+
+        make.into = into
+        return make
+
+    def at_y(p):
+        return (row, z * 4 + p)
+
+    def at_z(p):
+        return (row, p * 4 + 3)
+
+    y_step = lane("y_step", own_ref, y_near, at_y((y + 1) % 4), PARTS, RISE)
+    y_two = lane("y_two", y_all, y_far, at_y(2), PARTS, RISE)
+    y_three = lane("y_three", y_all, y_far, at_y(3), PARTS, RISE, y_two.into)
+    z_step = lane("z_step", y_all, z_near, at_z((z + 1) % 4), PARTS, RISE)
+    z_two = lane("z_two", z_all, z_far, at_z(2), PARTS, RISE)
+    z_three = lane("z_three", z_all, z_far, at_z(3), PARTS, RISE, z_two.into)
+    core_step = lane("core", z_all, core_near, (row + 1 - 2 * core, col), PARTS, RISE)
+    chain = lane("chain", x_next, x_in, (row + 2, col), TURNS, MEMBERS)
+    side = lane("side", x_in, x_row, (row + 1 - 2 * core, col), TURNS, MEMBERS)
+    z_out = [lane("z", x_row, x_z, at_z(0), TURNS, MEMBERS)]
+    z_out += [lane("z", x_row, x_z, at_z(p), TURNS, MEMBERS, z_out[0].into) for p in (1, 2)]
+    y_out = [lane("y", x_zs, x_y, at_y(0), TURNS, MEMBERS)]
+    y_out += [lane("y", x_zs, x_y, at_y(p), TURNS, MEMBERS, y_out[0].into) for p in (1, 2)]
 
     barrier = pltpu.get_barrier_semaphore()
 
@@ -214,12 +265,12 @@
         pl.semaphore_signal(barrier, inc=1, device_id=device, device_id_type=MESH)
 
     for k in range(1, 4):
-        greet((row, z * 4 + (y + k) % 4))
+        greet(at_y((y + k) % 4))
 
     @pl.when(y == 3)
     def _():
         for k in range(1, 4):
-            greet((row, ((z + k) % 4) * 4 + y))
+            greet(at_z((z + k) % 4))
 
     @pl.when(corner)
     def _():
@@ -238,91 +289,130 @@
     met = 3 + 3 * last_y + last * (1 + jnp.where(x > 0, 1, 0) + jnp.where(x < 3, 1, 0))
     pl.semaphore_wait(barrier, met)
 
-    def apply(later, state):
-        return exact(jnp.concatenate([later[0], later[1]], axis=1), state) + later[2]
-
-    def join(later, block, j):
-        got = exact(jnp.concatenate([later[0], later[1]], axis=1), block)
-        return got + later[2] if j == 2 else got
-
-    def level(place, at, own, near, far, pair, all_, base):
-        def near_copy(j, to):
-            return remote(own.at[j], near.at[j], base + j, base + j, at(to))
-
-        def far_copy(src, j, to, slot):
-            return remote(src.at[j], far.at[j], base + slot + j, base + 3 + j, at(to))
-
-        @pl.when(place == 0)
-        def _():
-            for j in range(3):
-                near_copy(j, 1).start()
-            for j in range(3):
-                far_copy(far, j, 3, 3).wait_recv()
-                far_copy(far, j, 3, 3).start()
-            for j in range(3):
-                near_copy(j, 1).wait_send()
-                far_copy(far, j, 3, 3).wait_send()
-
-        @pl.when(place == 1)
-        def _():
-            for j in range(3):
-                near_copy(j, 2).wait_recv()
-                all_[j] = join(own, near[j], j)
-                far_copy(all_, j, 2, 3).start()
-                far_copy(all_, j, 0, 6).start()
-            for j in range(3):
-                far_copy(all_, j, 2, 3).wait_send()
-                far_copy(all_, j, 0, 6).wait_send()
-
-        @pl.when(place == 2)
-        def _():
-            for j in range(3):
-                near_copy(j, 3).start()
-            for j in range(3):
-                far_copy(far, j, 3, 3).wait_recv()
-            for j in range(3):
-                near_copy(j, 3).wait_send()
-
-        @pl.when(place == 3)
-        def _():
-            for j in range(3):
-                near_copy(j, 2).wait_recv()
-                pair[j] = join(own, near[j], j)
-            for j in range(3):
-                far_copy(far, j, 2, 3).wait_recv()
-                all_[j] = join(pair, far[j], j)
-
-    level(y, lambda p: (row, z * 4 + p), own_ref, y_near, y_far, y_pair, y_all, 0)
+    def store_cut(slot, whole):
+        for i, part in enumerate(cut(whole[0:D, :])):
+            slot[i] = part
+
+    def times(block, slot):
+        size = block.shape[0]
+        high, middle, low = cut(block)
+        first = fast(jnp.concatenate([high, middle, low], axis=0), slot[0])
+        second = fast(jnp.concatenate([high, middle], axis=0), slot[1])
+        third = fast(high, slot[2])
+        small = first[2 * size:] + second[size:] + third
+        return first[:size] + (first[size:2 * size] + second[:size] + small)
+
+    def join(slot, later, earlier, k):
+        rows = pl.ds(RISE * k, RISE)
+        got = times(earlier[rows, :], slot)
+        return got + later[rows, :] if k >= MATRIX else got
+
+    def put(out, slot, later, earlier, k):
+        out[pl.ds(RISE * k, RISE), :] = join(slot, later, earlier, k)
+
+    def apply(slot, later, state, k):
+        rows = pl.ds(MEMBERS * k, MEMBERS)
+        return times(state[rows, :], slot) + later[pl.ds(D + MEMBERS * k, MEMBERS), :]
+
+    @pl.when(jnp.logical_or(y == 0, y == 2))
+    def _():
+        for k in range(PARTS):
+            y_step(k).start()
+
+    @pl.when(y == 1)
+    def _():
+        store_cut(own_cut, own_ref)
+        for k in range(PARTS):
+            y_step(k).wait_recv()
+            put(y_all, own_cut, own_ref, y_near, k)
+            y_three(k).start()
+            y_two(k).start()
+        store_cut(y_cut, y_near)
+
+    @pl.when(y == 2)
+    def _():
+        for k in range(PARTS):
+            y_two(k).wait_recv()
+        store_cut(y_cut, y_far)
 
     @pl.when(y == 3)
     def _():
-        level(z, lambda p: (row, p * 4 + 3), y_all, z_near, z_far, z_pair, z_all, 9)
-        for j in range(3):
-            y_pair[j] = join(y_near, y_far[j], j)
-
-    def core_copy(j):
-        return remote(z_all.at[j], core_near.at[j], 18 + j, 18 + j, (row + 1 - 2 * core, col))
-
-    def chain_copy():
-        return remote(x_z, x_in, 21, 21, (row + 2, col))
-
-    def back_copy():
-        return remote(x_in, x_row, 22, 22, (row + 1 - 2 * core, col))
-
-    def z_copy(to, slot):
-        return remote(x_row, x_z, slot, 23, (row, to * 4 + 3))
-
-    def y_copy(to, slot):
-        return remote(x_zs, x_y, slot, 24, (row, z * 4 + to))
+        def pair_y(k):
+            y_step(k).wait_recv()
+            put(y_pair, own_cut, own_ref, y_near, k)
+
+        def all_y(k):
+            y_two(k).wait_recv()
+            put(y_all, pair_cut, y_pair, y_far, k)
+
+            @pl.when(jnp.logical_or(z == 0, z == 2))
+            def _():
+                z_step(k).start()
+
+        def one_z(k):
+            z_step(k).wait_recv()
+            put(z_all, z_cut, y_all, z_near, k)
+            z_three(k).start()
+            z_two(k).start()
+
+        def pair_z(k):
+            z_step(k).wait_recv()
+            put(z_pair, z_cut, y_all, z_near, k)
+
+        store_cut(own_cut, own_ref)
+        for k in range(MATRIX):
+            pair_y(k)
+        store_cut(pair_cut, y_pair)
+        for k in range(MATRIX):
+            all_y(k)
+        for k in range(MATRIX, PARTS):
+            pair_y(k)
+
+        def between(parts):
+            @pl.when(z == 1)
+            def _():
+                for k in parts:
+                    one_z(k)
+
+            @pl.when(z == 3)
+            def _():
+                for k in parts:
+                    pair_z(k)
+
+        store_cut(z_cut, y_all)
+        between((0, 1))
+        all_y(MATRIX)
+        between((2,))
+        all_y(MATRIX + 1)
+        between((3, 4, 5))
+
+    def before_y():
+        store_cut(own_cut, y_near)
+        for k in range(PARTS):
+            put(y_before, own_cut, y_near, y_far, k)
+        store_cut(y_cut, y_before)
+
+    def before_z():
+        store_cut(own_cut, z_near)
+        for k in range(PARTS):
+            put(z_before, own_cut, z_near, z_far, k)
+        store_cut(z_cut, z_before)
 
     @pl.when(corner)
     def _():
+        store_cut(pair_cut, z_pair)
+        for k in range(PARTS):
+            z_two(k).wait_recv()
+            put(z_all, pair_cut, z_pair, z_far, k)
+
+            @pl.when(core == 0)
+            def _():
+                core_step(k).start()
+
         @pl.when(core == 0)
         def _():
-            for j in range(3):
-                core_copy(j).start()
-            for j in range(3):
-                z_pair[j] = join(z_near, z_far[j], j)
+            before_z()
+            before_y()
 
             @pl.when(x == 0)
             def _():
@@ -330,88 +420,163 @@
 
             @pl.when(x > 0)
             def _():
-                back_copy().wait_recv()
-
-            for j in range(3):
-                core_copy(j).wait_send()
+                for k in range(TURNS):
+                    side(k).wait_recv()
+                    for out in z_out:
+                        out(k).start()
+
+            @pl.when(x == 0)
+            def _():
+                for k in range(TURNS):
+                    for out in z_out:
+                        out(k).start()
 
         @pl.when(core == 1)
         def _():
-            for j in range(3):
-                core_copy(j).wait_recv()
-                core_all[j] = join(z_all, core_near[j], j)
-            for j in range(3):
-                z_pair[j] = join(z_near, z_far[j], j)
+            store_cut(core_cut, z_all)
+            for k in range(PARTS):
+                core_step(k).wait_recv()
+
+                @pl.when(x < 3)
+                def _():
+                    put(core_all, core_cut, z_all, core_near, k)
+
+            store_cut(side_cut, core_near)
+            store_cut(chain_cut, core_all)
 
             @pl.when(x == 0)
             def _():
                 x_in[...] = init_ref[...]
 
+            @pl.when(x >= 2)
+            def _():
+                before_z()
+                before_y()
+
+            for k in range(TURNS):
+                rows = pl.ds(MEMBERS * k, MEMBERS)
+
+                @pl.when(x > 0)
+                def _():
+                    chain(k).wait_recv()
+                    side(k).start()
+
+                @pl.when(x < 3)
+                def _():
+                    x_next[rows, :] = apply(chain_cut, core_all, x_in, k)
+                    chain(k).start()
+
+                x_row[rows, :] = apply(side_cut, core_near, x_in, k)
+                for out in z_out:
+                    out(k).start()
+
+            @pl.when(x < 2)
+            def _():
+                before_z()
+                before_y()
+
+        for k in range(TURNS):
+            x_zs[pl.ds(MEMBERS * k, MEMBERS), :] = apply(z_cut, z_before, x_row, k)
+            for out in y_out:
+                out(k).start()
+
+    @pl.when(jnp.logical_and(y == 3, z != 3))
+    def _():
+        @pl.when(z == 1)
+        def _():
+            store_cut(z_cut, z_near)
+
+        @pl.when(z == 2)
+        def _():
+            for k in range(PARTS):
+                z_two(k).wait_recv()
+            store_cut(z_cut, z_far)
+
+        before_y()
+        for k in range(TURNS):
+            rows = pl.ds(MEMBERS * k, MEMBERS)
+            z_out[0](k).wait_recv()
+
+            @pl.when(z == 0)
+            def _():
+                x_zs[rows, :] = x_z[rows, :]
+
+            @pl.when(z == 1)
+            def _():
+                x_zs[rows, :] = apply(z_cut, z_near, x_z, k)
+
+            @pl.when(z == 2)
+            def _():
+                x_zs[rows, :] = apply(z_cut, z_far, x_z, k)
+
+            for out in y_out:
+                out(k).start()
+
+    for k in range(TURNS):
+        rows = pl.ds(MEMBERS * k, MEMBERS)
+
+        @pl.when(y == 3)
+        def _():
+            start_ref[rows, :] = apply(y_cut, y_before, x_zs, k)
+
+        @pl.when(y != 3)
+        def _():
+            y_out[0](k).wait_recv()
+
+            @pl.when(y == 0)
+            def _():
+                start_ref[rows, :] = x_y[rows, :]
+
+            @pl.when(y == 1)
+            def _():
+                start_ref[rows, :] = apply(y_cut, y_near, x_y, k)
+
+            @pl.when(y == 2)
+            def _():
+                start_ref[rows, :] = apply(y_cut, y_far, x_y, k)
+
+    def sent(parts, *lanes):
+        for one in lanes:
+            for k in range(parts):
+                one(k).wait_send()
+
+    @pl.when(jnp.logical_or(y == 0, y == 2))
+    def _():
+        sent(PARTS, y_step)
+
+    @pl.when(y == 1)
+    def _():
+        sent(PARTS, y_two, y_three)
+
+    @pl.when(y == 3)
+    def _():
+        sent(TURNS, *y_out)
+
+        @pl.when(jnp.logical_or(z == 0, z == 2))
+        def _():
+            sent(PARTS, z_step)
+
+        @pl.when(z == 1)
+        def _():
+            sent(PARTS, z_two, z_three)
+
+    @pl.when(corner)
+    def _():
+        sent(TURNS, *z_out)
+
+        @pl.when(core == 0)
+        def _():
+            sent(PARTS, core_step)
+
+        @pl.when(core == 1)
+        def _():
             @pl.when(x > 0)
             def _():
-                chain_copy().wait_recv()
-                back_copy().start()
+                sent(TURNS, side)
 
             @pl.when(x < 3)
             def _():
-                x_z[...] = apply(core_all, x_in[...])
-                chain_copy().start()
-
-            x_row[...] = apply(core_near, x_in[...])
-
-            @pl.when(x > 0)
-            def _():
-                back_copy().wait_send()
-
-            @pl.when(x < 3)
-            def _():
-                chain_copy().wait_send()
-
-        for to in range(3):
-            z_copy(to, 22 + 1 + to).start()
-        x_zs[...] = apply(z_pair, x_row[...])
-        for to in range(3):
-            z_copy(to, 22 + 1 + to).wait_send()
-
-    @pl.when(jnp.logical_and(y == 3, z != 3))
-    def _():
-        z_copy(0, 23).wait_recv()
-
-        @pl.when(z == 0)
-        def _():
-            x_zs[...] = x_z[...]
-
-        @pl.when(z == 1)
-        def _():
-            x_zs[...] = apply(z_near, x_z[...])
-
-        @pl.when(z == 2)
-        def _():
-            x_zs[...] = apply(z_far, x_z[...])
-
-    @pl.when(y == 3)
-    def _():
-        for to in range(3):
-            y_copy(to, 26 + to).start()
-        start_ref[...] = apply(y_pair, x_zs[...])
-        for to in range(3):
-            y_copy(to, 26 + to).wait_send()
-
-    @pl.when(y != 3)
-    def _():
-        y_copy(0, 26).wait_recv()
-
-        @pl.when(y == 0)
-        def _():
-            start_ref[...] = x_y[...]
-
-        @pl.when(y == 1)
-        def _():
-            start_ref[...] = apply(y_near, x_y[...])
-
-        @pl.when(y == 2)
-        def _():
-            start_ref[...] = apply(y_far, x_y[...])
+                sent(TURNS, chain)
 
 
 def carried_in(root, initial):
@@ -420,12 +585,13 @@
         scan_kernel,
         in_specs=[whole, whole],
         out_specs=whole,
-        out_shape=jax.ShapeDtypeStruct((D, E), F32),
-        scratch_shapes=[VMEM((3, D, E), F32)] * 10
-        + [VMEM((D, E), F32)] * 5
-        + [pltpu.SemaphoreType.DMA((29,)), pltpu.SemaphoreType.DMA((25,))],
+        out_shape=jax.ShapeDtypeStruct((E, D), F32),
+        scratch_shapes=[VMEM((WIDE, D), F32)] * 12
+        + [VMEM((E, D), F32)] * 6
+        + [VMEM((3, D, D), BF16)] * 7
+        + [pltpu.SemaphoreType.DMA((74,)), pltpu.SemaphoreType.DMA((46,))],
         compiler_params=pltpu.CompilerParams(
-            collective_id=0, has_side_effects=True, vmem_limit_bytes=16 * 1024 * 1024
+            collective_id=0, has_side_effects=True, vmem_limit_bytes=24 * 1024 * 1024
         ),
     )(root, initial)
 
@@ -446,7 +612,7 @@
         return exact(later[:, :D], value) + later[:, D:]
 
     begin = [None] * groups
-    begin[0] = start_ref[...]
+    begin[0] = start_ref[...].T
     begin[2] = apply(top_ref[2], begin[0])
     begin[1] = apply(top_ref[0], begin[0])
     begin[3] = apply(top_ref[1], begin[2])
@@ -518,7 +684,7 @@
     mask_t = mask.T
     row = weights.reshape(1, OBS)
     left, top, root = local_maps(mask_t, observed, obs_map, row, transition)
-    start = carried_in(root, initial)
+    start = carried_in(root, initial.T)
     return means_of(start, left, top, mask_t, observed, obs_map, row, transition)
 
 

time: 129 us -> 105 us (0.81)
  Pallas kernels: 122 us -> 99.2 us
    pallas_call x1, Pallas kernels: 69.6 us -> 44.8 us  [carried_in(): pl.pallas_call(scan_kernel, in_specs=[whole, whole], out_specs=whole, out...]
    pallas_call x1, Pallas kernels: 25.8 us -> 27.6 us  [local_maps(): pl.pallas_call(maps_kernel, grid=(turns,), in_specs=[whole((OBS, steps)),...]
    unnamed x10 -> x9, local copies, waits for them, and re-layouts: 4.1 us -> 4.19 us
where the time goes in v2:
time: 105 us; the launch traced here: 104 us
  Pallas kernels  99.2 us (94%)
  local copies, waits for them, and re-layouts  4.19 us (4%)
    pallas_call x1, Pallas kernels, carried_in(): pl.pallas_call(scan_kernel, in_specs=[whole, whole], out_specs=whole, out...  44.8 us
    pallas_call x1, Pallas kernels, local_maps(): pl.pallas_call(maps_kernel, grid=(turns,), in_specs=[whole((OBS, steps)),...  27.6 us
    pallas_call x1, Pallas kernels, means_of(): pl.pallas_call(means_kernel, in_specs=[whole] * 8, out_specs=pl.BlockSpec...  26.8 us
    unnamed x9, local copies, waits for them, and re-layouts  4.19 us

profile of v2, /device:TPU:6, one launch (start us, length us, event | category | flops | bytes accessed | tf_op | source)
XLA Modules:
  0.0 103.6 jit_solution(13442736432698169784)
XLA Ops:
  0.0 1.0 copy.7
  1.0 0.0 copy-start
  1.0 0.9 copy-done
  2.0 0.0 copy-start.1
  2.0 0.8 copy-done.1
  2.8 0.0 copy-start.2
  2.8 0.8 copy-done.2
  3.6 0.0 copy-start.3
  3.6 0.7 copy-done.3
  4.2 27.6 %shard_map.64 = (f32[4,3,256,384]{3,2,1,0:T(8,128)}, f32[3,256,384]{2,1,0:T(8,128)S(1)}, f32[384,256]{1,0:T(8,128)S(1)}) custom-call(s32[64,128]{1,0:T(8,128)S(1)} %bitcast.5, f32[128,64,128]{2,1,0:T(8,128)} %obs_ref.3, f32[64,256]{1,0:T(8,128)S(1)} %copy-done.1, f32[1,64]{1,0:T(1,128)S(1)} %bitcast.7, f32[256,256]{1,0:T(8,128)S(1)} %copy-done), custom_call_target="tpu_custom_call" | custom-call | tf_op jit(solution)/shard_map/pallas_call | solution.py:163
  31.8 44.8 %shard_map.65.start_ref = f32[128,256]{1,0:T(8,128)S(1)} custom-call(f32[384,256]{1,0:T(8,128)S(1)} %get-tuple-element.8.own_ref, f32[128,256]{1,0:T(8,128)S(1)} %bitcast.4), custom_call_target="tpu_custom_call" | custom-call | tf_op jit(solution)/shard_map/pallas_call | solution.py:584
  76.6 26.8 %shard_map.66 = f32[16,8,256,128]{3,2,1,0:T(8,128)} custom-call(f32[128,256]{1,0:T(8,128)S(1)} %shard_map.65.start_ref, f32[4,3,256,384]{3,2,1,0:T(8,128)} %get-tuple-element.9.left_ref, f32[3,256,384]{2,1,0:T(8,128)S(1)} %get-tuple-element.10.top_ref, s32[64,128]{1,0:T(8,128)S(1)} %bitcast.6, f32[128,64,128]{2,1,0:T(8,128)} %obs_ref.3, ...), custom_call_target="tpu_custom_call" | custom-call | tf_op jit(solution)/shard_map/pallas_call | solution.py:665
Async XLA Ops:
  1.0 1.0 copy-start
  2.0 0.8 copy-start.1
  2.8 0.8 copy-start.2
  3.6 0.7 copy-start.3
